TPU v7x, 32 devices: a whole 2x2x4 slice. The times are simulated.
32 devices in a mesh: gx: 4 (over x, core), gy: 2 (over y), gz: 4 (over z).
Axes of the slice: x: 2, y: 2, z: 4, core: 2. Of those that a mesh axis runs over, the one named last changes fastest.
Arguments:
- energy: float32 [24, 24, 768], P('gx', 'gy', 'gz'), may hold values from 0.5 to 18, as said below
- density: float32 [8, 8, 256], P('gx', 'gy', 'gz'), may hold values from 0.125 to 1
- region: int32 [8, 8, 256], P('gx', 'gy', 'gz'), may hold values from 0 to 2
- gamma_table: float32 [3], replicated, may hold values from 1.3 to 1.9
Outputs:
- acceleration: float32 [3, 16, 16, 512], P(None, 'gx', 'gy', 'gz')
- residual: float32 [3, 16, 16, 512], P(None, 'gx', 'gy', 'gz')
Inputs may be any that keep to these rules, and one draw needn't show every extreme that they name: energy is positive.
All inputs are finite; a program needn't handle non-finite values.
Results may differ from a plain program's by a relative error of at most 0.0001.
Values sent between devices are 32-bit elements; how exact they have to be, the bound alone decides.
A program may use at most 64 MiB of HBM per device.

v0:
```python
import functools
import math

import jax
import jax.numpy as jnp
import numpy as np
from jax import lax
from jax.experimental import pallas as pl
from jax.experimental.pallas import tpu as pltpu
from jax.sharding import PartitionSpec as P

MESH = pl.DeviceIdType.MESH
AXES = ("gx", "gy", "gz")
WEIGHTS = [5.0 / 18.0, 8.0 / 18.0, 5.0 / 18.0]
SUB = 8
PHASES = 3


def line_tables():
    root = math.sqrt(0.15)
    spots = [0.5 - root, 0.5, 0.5 + root]
    values = [
        [2.0 * (spot - 0.5) * (spot - 1.0), -4.0 * spot * (spot - 1.0), 2.0 * spot * (spot - 0.5)]
        for spot in spots
    ]
    slopes = [[4.0 * spot - 3.0, -8.0 * spot + 4.0, 4.0 * spot - 1.0] for spot in spots]
    return np.array(values), np.array(slopes)


def line_mass():
    values, _ = line_tables()
    return values.T @ np.diag(WEIGHTS) @ values


def z_matrix(cz, lanes):
    values, slopes = line_tables()
    out = np.zeros((3 * cz, 6, lanes), np.float32)
    for k in range(3):
        for a in range(3):
            for e in range(cz):
                out[3 * e + a, k, e] = WEIGHTS[a] * values[a][k]
                out[3 * e + a, 3 + k, e] = WEIGHTS[a] * slopes[a][k]
    return out.reshape(3 * cz, 6 * lanes)


def line_matrix(count, table):
    out = np.zeros((2 * count + 1, 3 * count))
    for i in range(count):
        for a in range(3):
            for k in range(3):
                out[2 * i + k, 3 * i + a] += WEIGHTS[a] * table[a][k]
    return out


def plane_matrix(cx, cy):
    values, slopes = line_tables()
    vx, sx = line_matrix(cx, values), line_matrix(cx, slopes)
    vy, sy = line_matrix(cy, values), line_matrix(cy, slopes)
    nx, ny, points = 2 * cx + 1, 2 * cy + 1, 9 * cx * cy
    out = np.zeros((ny, nx, SUB, 2, points), np.float32)
    for c, (mx, my, part) in enumerate(((sx, vy, 0), (vx, sy, 0), (vx, vy, 1))):
        block = np.einsum("xp,yq->yxpq", mx, my).reshape(ny, nx, points)
        out[:, :, c, part] = block
        out[:, :, c + 4, part] = block
    return out.reshape(ny * nx * SUB, 2 * points)


def weave_matrix(cz, lanes):
    out = np.zeros((2, lanes, 2 * cz), np.float32)
    for e in range(cz):
        out[0, e, 2 * e] = 1.0
        out[1, e, 2 * e + 1] = 1.0
    return out.reshape(2 * lanes, 2 * cz)


def exact_dot(a, b):
    return jnp.dot(a, b, precision=lax.Precision.HIGHEST, preferred_element_type=jnp.float32)


def reduction_stages(sizes):
    if math.prod(sizes) <= 64:
        return [(0, 1, 2)]
    return [(0,), (1,), (2,)]


def group_size(stage, sizes):
    return math.prod(sizes[axis] for axis in stage)


def axis_directions(index, size):
    if size == 1:
        return []
    if size == 2:
        return [(0, 0, 1 - 2 * index, None)]
    return [(0, 1, -1, index > 0), (1, 0, 1, index < size - 1)]


def pick(step, low, high):
    if isinstance(step, int):
        return low if step < 0 else high
    return jnp.where(step > 0, high, low)


def under(conditions, action):
    conditions = [c for c in conditions if c is not None]
    if not conditions:
        action()
        return
    both = conditions[0]
    for c in conditions[1:]:
        both = jnp.logical_and(both, c)
    pl.when(both)(action)


def kernel(
    sizes, cx, cy, cz, lanes,
    energy, density, region, gamma, z_mat, plane_mat, weave_mat,
    acc_out, res_out,
    points, fac, fac_points, dens, part, full, rows, z_part, x_buf, y_buf, xy_buf, z_buf,
    send_sem, recv_sem, *stage_refs,
):
    nx, ny = 2 * cx + 1, 2 * cy + 1
    nodes = nx * ny
    place = [lax.axis_index(name) for name in AXES]
    stages = reduction_stages(sizes)
    centre = (2, 2, 0, None)
    dirs = [axis_directions(place[axis], sizes[axis]) for axis in range(3)]
    sides = [d + [centre] for d in dirs]

    def target(step_x, step_y, step_z):
        return (place[0] + step_x, place[1] + step_y, place[2] + step_z)

    def partner(stage, offset):
        mine = 0
        for axis in stage:
            mine = mine * sizes[axis] + place[axis]
        other = lax.rem(mine + offset, group_size(stage, sizes))
        where = list(place)
        for axis in reversed(stage):
            where[axis] = lax.rem(other, sizes[axis])
            other = lax.div(other, sizes[axis])
        return tuple(where), mine

    for ref in (x_buf, y_buf, xy_buf, z_buf):
        ref[...] = jnp.zeros_like(ref)

    barrier = pltpu.get_barrier_semaphore()
    for stage in stages:
        size = group_size(stage, sizes)

        @pl.loop(1, size)
        def _(offset, stage=stage):
            where, _mine = partner(stage, offset)
            pl.semaphore_signal(barrier, inc=1, device_id=where, device_id_type=MESH)

    for xp in range(3 * cx):
        points[pl.ds(xp * 3 * cy, 3 * cy), :] = energy[xp]
    gamma_elem = jnp.zeros(region.shape, jnp.float32)
    for index in range(gamma.shape[0]):
        gamma_elem = gamma_elem + jnp.where(region[...] == index, gamma[index], 0.0)
    factor = (gamma_elem - 1.0) * density[...]
    fac[...] = jnp.zeros_like(fac)
    dens[...] = jnp.zeros_like(dens)
    for i in range(cx):
        fac[pl.ds(i * cy, cy), pl.ds(0, cz)] = factor[i]
        dens[pl.ds(i * cy, cy), pl.ds(0, cz)] = density[i]
    for xp in range(3 * cx):
        for k in range(cy):
            row = fac[pl.ds((xp // 3) * cy + k, 1), :]
            fac_points[pl.ds(xp * 3 * cy + 3 * k, 3), :] = jnp.broadcast_to(row, (3, lanes))
    sums = exact_dot(points[...], z_mat[...])
    scaled = [sums[:, k * lanes : (k + 1) * lanes] * fac_points[...] for k in range(6)]
    even = jnp.concatenate(
        [scaled[0] + pltpu.roll(scaled[2], 1, 1), scaled[3] + pltpu.roll(scaled[5], 1, 1)], axis=0
    )
    odd = jnp.concatenate([scaled[1], scaled[4]], axis=0)
    force = exact_dot(plane_mat[...], jnp.concatenate([even, odd], axis=1))
    sub = lax.broadcasted_iota(jnp.int32, (1, SUB, lanes), 1)
    lane = lax.broadcasted_iota(jnp.int32, (1, SUB, lanes), 2)
    is_even = sub < 4
    e_part = force[:, :lanes].reshape(nodes, SUB, lanes)
    o_part = force[:, lanes:].reshape(nodes, SUB, lanes)
    part[0] = jnp.where(is_even, e_part, o_part).reshape(ny, nx, SUB, lanes)

    used = jnp.logical_and(lax.rem(sub, 4) < 3, lane < jnp.where(is_even, cz + 1, cz))
    wall_low = jnp.logical_and(place[2] == 0, jnp.logical_and(is_even, lane == 0))
    wall_high = jnp.logical_and(
        place[2] == sizes[2] - 1, jnp.logical_and(is_even, lane == cz)
    )
    keep = jnp.where(
        jnp.logical_and(used, jnp.logical_not(jnp.logical_or(wall_low, wall_high))), 1.0, 0.0
    )
    owned = jnp.where(lane < cz, 1.0, 0.0)
    ends = [jnp.logical_and(is_even, lane == 0), jnp.logical_and(is_even, lane == cz)]
    spot = lax.broadcasted_iota(jnp.int32, (nodes, SUB, 128), 0)
    pack_lane = lax.broadcasted_iota(jnp.int32, (nodes, SUB, 128), 2)
    pack_hot = jnp.where(spot == pack_lane, 1.0, 0.0)
    flat_lane = lax.broadcasted_iota(jnp.int32, (SUB, 128), 1)
    lane_x, lane_y = lax.rem(flat_lane, nx), lax.div(flat_lane, nx)

    def copies(phase, side_x, side_y, side_z):
        (sx, tx, dx, _), (sy, ty, dy, _), (sz, tz, dz, _) = side_x, side_y, side_z
        here, there = [phase * 27 + (a * 3 + b) * 3 + c for a, b, c in ((sx, sy, sz), (tx, ty, tz))]
        xf, yf = pick(dx, 0, nx - 1), pick(dy, 0, ny - 1)
        if sz != 2:
            src = z_part.at[phase, pick(dz, 0, 1)]
            dst, own = z_buf.at[phase, tz, tx, ty], z_buf.at[phase, sz, sx, sy]
        elif sy == 2:
            src = part.at[phase, :, xf]
            dst, own = x_buf.at[phase, tx], x_buf.at[phase, sx]
        elif sx == 2:
            src = part.at[phase, yf]
            dst, own = y_buf.at[phase, ty], y_buf.at[phase, sy]
        else:
            src = part.at[phase, yf, xf]
            dst, own = xy_buf.at[phase, tx, ty], xy_buf.at[phase, sx, sy]

        def make(dst_ref, slot):
            return pltpu.make_async_remote_copy(
                src_ref=src, dst_ref=dst_ref, send_sem=send_sem.at[here], recv_sem=recv_sem.at[slot],
                device_id=target(dx, dy, dz), device_id_type=MESH,
            )

        return lambda: make(dst, there), lambda: make(own, here)

    def each(phase, plane, action):
        groups = {}
        for side_z in [centre] if plane else dirs[2]:
            for side_x in sides[0]:
                for side_y in sides[1]:
                    if side_z[0] == 2 and side_x[0] == 2 and side_y[0] == 2:
                        continue
                    conditions = (side_x[3], side_y[3], side_z[3])
                    key = tuple(None if c is None else s[0] for c, s in zip(conditions, (side_x, side_y, side_z)))
                    groups.setdefault(key, (conditions, []))[1].append((side_x, side_y, side_z))
        for conditions, members in groups.values():

            def run(members=members):
                for member in members:
                    action(copies(phase, *member))

            under(conditions, run)

    def start(phase):
        each(phase, True, lambda pair: pair[0]().start())
        whole = part[phase].reshape(nodes, SUB, lanes)
        for side, at in ((0, 0), (1, cz)):
            z_part[phase, side] = jnp.sum(whole[:, :, at : at + 1] * pack_hot, axis=0)
        each(phase, False, lambda pair: pair[0]().start())

    def finish(phase):
        each(phase, True, lambda pair: pair[1]().wait_recv())
        full[phase] = part[phase]
        for sx, _, dx, _ in dirs[0]:
            xf = pick(dx, 0, nx - 1)
            full[phase, :, xf] = full[phase, :, xf] + x_buf[phase, sx]
        for sy, _, dy, _ in dirs[1]:
            yf = pick(dy, 0, ny - 1)
            full[phase, yf] = full[phase, yf] + y_buf[phase, sy]
            for sx, _, dx, _ in dirs[0]:
                xf = pick(dx, 0, nx - 1)
                full[phase, yf, xf] = full[phase, yf, xf] + xy_buf[phase, sx, sy]
        each(phase, False, lambda pair: pair[1]().wait_recv())
        whole = full[phase].reshape(nodes, SUB, lanes)
        for sz, _, dz, _ in dirs[2]:
            tile = z_buf[phase, sz, 2, 2]
            for sx, _, dx, _ in sides[0]:
                for sy, _, dy, _ in sides[1]:
                    if sx == 2 and sy == 2:
                        continue
                    moved = pltpu.roll(
                        z_buf[phase, sz, sx, sy],
                        lax.rem(dx * (nx - 1) + dy * (ny - 1) * nx + 128, 128), 1,
                    )
                    good = flat_lane < nodes
                    if sx != 2:
                        good = jnp.logical_and(good, lane_x == pick(dx, 0, nx - 1))
                    if sy != 2:
                        good = jnp.logical_and(good, lane_y == pick(dy, 0, ny - 1))
                    tile = tile + jnp.where(good, moved, 0.0)
            spread = jnp.sum(tile[None] * pack_hot, axis=2, keepdims=True)
            end = pick(dz, ends[0], ends[1])
            whole = whole + jnp.where(end, spread, 0.0)
        full[phase] = (whole * keep).reshape(ny, nx, SUB, lanes)
        for axis, last in ((0, nx - 1), (1, ny - 1)):
            for at, here in ((0, place[axis] == 0), (last, place[axis] == sizes[axis] - 1)):

                @pl.when(here)
                def _(axis=axis, at=at):
                    if axis == 0:
                        full[phase, :, at] = jnp.zeros((ny, SUB, lanes), jnp.float32)
                    else:
                        full[phase, at] = jnp.zeros((nx, SUB, lanes), jnp.float32)

    mass = [[float(v) for v in line] for line in line_mass()]

    def combine(weights, parts):
        return weights[0] * parts[0] + weights[1] * parts[1] + weights[2] * parts[2]

    on_even, on_odd, on_next = [
        jnp.where(is_even, mass[0][k], mass[1][k]).astype(jnp.float32) for k in range(3)
    ]
    even_only = jnp.where(is_even, 1.0, 0.0)

    def apply_mass(source, phase):
        lines = [full[source, y] for y in range(ny)]
        along_y = jnp.concatenate(
            [combine(mass[l], lines[2 * k : 2 * k + 3])[None] for k in range(cy) for l in range(3)],
            axis=0,
        )
        at_x = [along_y[:, x] for x in range(nx)]
        blocks = []
        for i in range(cx):
            tiles = [
                jnp.broadcast_to(dens[pl.ds(i * cy + k, 1), :], (SUB, lanes))[None]
                for k in range(cy)
                for _ in range(3)
            ]
            rho = jnp.concatenate(tiles, axis=0)
            rho_next = rho * even_only
            for j in range(3):
                t = combine(mass[j], at_x[2 * i : 2 * i + 3])
                other = pltpu.roll(t, 4, 1)
                evens, odds = jnp.where(is_even, t, other), jnp.where(is_even, other, t)
                following = pltpu.roll(evens, lanes - 1, 2)
                own = on_even * evens + on_odd * odds + on_next * following
                far = combine(mass[2], (evens, odds, following))
                blocks.append(rho * own + pltpu.roll(rho_next * far, 1, 2))
        for x in range(nx):
            i, odd_x = divmod(x, 2)
            if odd_x:
                column = blocks[3 * i + 1]
            elif x == 0:
                column = blocks[0]
            elif x == nx - 1:
                column = blocks[3 * i - 1]
            else:
                column = blocks[3 * i] + blocks[3 * i - 1]
            for y in range(ny):
                k, odd_y = divmod(y, 2)
                if odd_y:
                    value = column[3 * k + 1]
                elif y == 0:
                    value = column[0]
                elif y == ny - 1:
                    value = column[3 * k - 1]
                else:
                    value = column[3 * k] + column[3 * k - 1]
                part[phase, y, x] = value

    def woven(phase):
        rows[...] = full[phase].reshape(nodes * SUB, lanes)
        halves = []
        for first in (0, 4):
            halves.append(jnp.concatenate(
                [
                    rows[pl.ds(x * SUB + first + c, 2 * cy, stride=nx * SUB), :]
                    for c in range(3)
                    for x in range(2 * cx)
                ],
                axis=0,
            ))
        return exact_dot(jnp.concatenate(halves, axis=1), weave_mat[...])

    if sum(group_size(stage, sizes) - 1 for stage in stages):
        pl.semaphore_wait(barrier, sum(group_size(stage, sizes) - 1 for stage in stages))
    start(0)
    finish(0)
    apply_mass(0, 1)
    start(1)
    finish(1)
    apply_mass(1, 2)
    start(2)

    force_own = full[0, : ny - 1, : nx - 1].reshape(4 * cx * cy, SUB, lanes) * owned
    image_own = full[1, : ny - 1, : nx - 1].reshape(4 * cx * cy, SUB, lanes) * owned
    products = [
        jnp.sum(force_own * force_own, axis=0),
        jnp.sum(force_own * image_own, axis=0),
        jnp.sum(image_own * image_own, axis=0),
        jnp.sum((full[1] * part[2]).reshape(nodes, SUB, lanes), axis=0),
    ]
    flat_sub = lax.broadcasted_iota(jnp.int32, (SUB, 128), 0)
    message = jnp.zeros((SUB, 128), jnp.float32)
    for k, product in enumerate(products):
        hot = flat_lane == 4 * lax.rem(flat_sub, 4) + k
        message = message + jnp.where(hot, jnp.sum(product, axis=1, keepdims=True), 0.0)
    total = jnp.sum(message, axis=0, keepdims=True)

    woven_force, woven_image = None, None
    for number, stage in enumerate(stages):
        slots, stage_send, stage_recv = stage_refs[3 * number : 3 * number + 3]
        size = group_size(stage, sizes)
        if size == 1:
            continue
        _, mine = partner(stage, 0)
        slots[mine] = total

        @pl.loop(1, size)
        def _(offset, stage=stage, slots=slots, stage_send=stage_send, stage_recv=stage_recv):
            where, at = partner(stage, offset)
            pltpu.make_async_remote_copy(
                src_ref=slots.at[at], dst_ref=slots.at[at],
                send_sem=stage_send, recv_sem=stage_recv,
                device_id=where, device_id_type=MESH,
            ).start()

        if number == 0:
            woven_force, woven_image = woven(0), woven(1)
            finish(2)
        where, _ = partner(stage, 1)
        others = slots.at[pl.ds(0, size - 1)]
        wait = pltpu.make_async_remote_copy(
            src_ref=others, dst_ref=others, send_sem=stage_send, recv_sem=stage_recv,
            device_id=where, device_id_type=MESH,
        )
        wait.wait_recv()
        wait.wait_send()
        total = jnp.sum(slots[...], axis=0)
    if woven_force is None:
        woven_force, woven_image = woven(0), woven(1)
        finish(2)
    woven_second = woven(2)

    row_lane = lax.broadcasted_iota(jnp.int32, (1, 128), 1)
    live = jnp.logical_and(lax.rem(row_lane, 4) == 0, row_lane < 12)
    ff, fi, ii, si = [
        jnp.where(live, total if k == 0 else pltpu.roll(total, 128 - k, 1), 1.0) for k in range(4)
    ]
    alpha = ff / fi
    next_norm = alpha * alpha * ii - ff
    ratio = next_norm / ff
    curvature = fi - 2.0 * alpha * ii + alpha * alpha * si - ratio * next_norm / alpha
    second = next_norm / curvature
    outer = alpha + second * (1.0 + ratio)
    inner = alpha * second
    per = 2 * cx * 2 * cy
    for c in range(3):
        hot = row_lane == 4 * c
        a = jnp.sum(jnp.where(hot, outer, 0.0), axis=1, keepdims=True)
        b = jnp.sum(jnp.where(hot, inner, 0.0), axis=1, keepdims=True)
        here = slice(c * per, (c + 1) * per)
        f, q, s = woven_force[here], woven_image[here], woven_second[here]
        acc_out[c] = (a * f - b * q).reshape(2 * cx, 2 * cy, 2 * cz)
        res_out[c] = (f - a * q + b * s).reshape(2 * cx, 2 * cy, 2 * cz)

    for phase in range(PHASES):
        each(phase, True, lambda pair: pair[0]().wait_send())
        each(phase, False, lambda pair: pair[0]().wait_send())


def solution(mesh):
    sizes = tuple(mesh.shape[name] for name in AXES)

    def on_device(energy, density, region, gamma_table):
        cx, cy, cz = density.shape
        lanes = -(-(cz + 1) // 128) * 128
        nx, ny = 2 * cx + 1, 2 * cy + 1
        out = jax.ShapeDtypeStruct((3, 2 * cx, 2 * cy, 2 * cz), jnp.float32)
        vmem = pl.BlockSpec(memory_space=pltpu.VMEM)
        tile = (SUB, lanes)
        scratch = [
            pltpu.VMEM((9 * cx * cy, 3 * cz), jnp.float32),
            pltpu.VMEM((cx * cy, lanes), jnp.float32),
            pltpu.VMEM((9 * cx * cy, lanes), jnp.float32),
            pltpu.VMEM((cx * cy, lanes), jnp.float32),
            pltpu.VMEM((PHASES, ny, nx) + tile, jnp.float32),
            pltpu.VMEM((PHASES, ny, nx) + tile, jnp.float32),
            pltpu.VMEM((ny * nx * SUB, lanes), jnp.float32),
            pltpu.VMEM((PHASES, 2, SUB, 128), jnp.float32),
            pltpu.VMEM((PHASES, 2, ny) + tile, jnp.float32),
            pltpu.VMEM((PHASES, 2, nx) + tile, jnp.float32),
            pltpu.VMEM((PHASES, 2, 2) + tile, jnp.float32),
            pltpu.VMEM((PHASES, 2, 3, 3, SUB, 128), jnp.float32),
            pltpu.SemaphoreType.DMA((PHASES * 27,)),
            pltpu.SemaphoreType.DMA((PHASES * 27,)),
        ]
        for stage in reduction_stages(sizes):
            scratch += [
                pltpu.VMEM((group_size(stage, sizes), 1, 128), jnp.float32),
                pltpu.SemaphoreType.DMA,
                pltpu.SemaphoreType.DMA,
            ]
        return pl.pallas_call(
            functools.partial(kernel, sizes, cx, cy, cz, lanes),
            out_shape=(out, out),
            in_specs=[vmem] * 3 + [pl.BlockSpec(memory_space=pltpu.SMEM)] + [vmem] * 3,
            out_specs=(vmem, vmem),
            scratch_shapes=scratch,
            compiler_params=pltpu.CompilerParams(
                collective_id=0, has_side_effects=True, vmem_limit_bytes=32 * 1024 * 1024
            ),
        )(
            energy, density, region, gamma_table,
            jnp.asarray(z_matrix(cz, lanes)),
            jnp.asarray(plane_matrix(cx, cy)),
            jnp.asarray(weave_matrix(cz, lanes)),
        )

    in_specs = (P(*AXES), P(*AXES), P(*AXES), P())
    out_specs = (P(None, *AXES), P(None, *AXES))
    return jax.shard_map(
        on_device, mesh=mesh, in_specs=in_specs, out_specs=out_specs, check_vma=False
    )
```

profile of v0, /device:TPU:0, one launch (start us, length us, event | category | flops | bytes accessed | tf_op | source)
XLA Modules:
  0.0 29.6 jit_solution(8887511343217699979)
XLA Ops:
  0.6 0.0 copy-start
  0.6 1.1 %copy-done = f32[192,768]{1,0:T(8,128)S(1)} copy-done((f32[192,768]{1,0:T(8,128)S(1)}, f32[192,768]{1,0:T(8,128)}, u32[]{:S(2)}) %copy-start) | copy-done | bytes 589848
  1.7 0.0 copy-start.1
  1.7 1.0 %copy-done.1 = f32[360,144]{1,0:T(8,128)S(1)} copy-done((f32[360,144]{1,0:T(8,128)S(1)}, f32[360,144]{1,0:T(8,128)}, u32[]{:S(2)}) %copy-start.1) | copy-done | bytes 207384
  2.7 0.0 copy-start.2
  2.7 0.9 %copy-done.2 = f32[256,128]{1,0:T(8,128)S(1)} copy-done((f32[256,128]{1,0:T(8,128)S(1)}, f32[256,128]{1,0:T(8,128)}, u32[]{:S(2)}) %copy-start.2) | copy-done | bytes 131096
  3.6 0.0 copy-start.3
  3.6 0.9 %copy-done.3 = f32[6,12,192]{2,1,0:T(8,128)S(1)} copy-done((f32[6,12,192]{2,1,0:T(8,128)S(1)}, f32[6,12,192]{2,1,0:T(8,128)}, u32[]{:S(2)}) %copy-start.3) | copy-done | bytes 55320
  4.5 0.0 copy-start.4
  4.5 0.7 %copy-done.4 = f32[2,4,64]{2,1,0:T(4,128)S(1)} copy-done((f32[2,4,64]{2,1,0:T(4,128)S(1)}, f32[2,4,64]{2,1,0:T(4,128)}, u32[]{:S(2)}) %copy-start.4) | copy-done | bytes 2072
  5.2 0.0 copy-start.5
  5.2 0.7 %copy-done.5 = s32[2,4,64]{2,1,0:T(4,128)S(1)} copy-done((s32[2,4,64]{2,1,0:T(4,128)S(1)}, s32[2,4,64]{2,1,0:T(4,128)}, u32[]{:S(2)}) %copy-start.5) | copy-done | bytes 2072
  5.9 0.0 copy-start.6
  5.9 0.7 %copy-done.6 = f32[3]{0:T(128)S(1)} copy-done((f32[3]{0:T(128)S(1)}, f32[3]{0:T(128)}, u32[]{:S(2)}) %copy-start.6) | copy-done | bytes 36
  6.5 21.8 %shard_map.86 = (f32[3,4,8,128]{3,2,1,0:T(8,128)S(1)}, f32[3,4,8,128]{3,2,1,0:T(8,128)S(1)}) custom-call(f32[6,12,192]{2,1,0:T(8,128)S(1)} %copy-done.3, f32[2,4,64]{2,1,0:T(4,128)S(1)} %copy-done.4, s32[2,4,64]{2,1,0:T(4,128)S(1)} %copy-done.5, f32[3]{0:T(128)S(1)} %copy-done.6, f32[192,768]{1,0:T(8,128)S(1)} %copy-done, f32[360,144]{1,0:T(8,128)S(1)} %copy-done.1, ...), custom_call_target="tpu_custom_call" | custom-call | tf_op jit(solution)/shard_map/pallas_call | solution.py:484
  28.3 0.6 %copy.11 = f32[3,4,8,128]{3,2,1,0:T(8,128)} copy(f32[3,4,8,128]{3,2,1,0:T(8,128)S(1)} %get-tuple-element.4) | data formatting | bytes 98304
  29.0 0.6 %copy.12 = f32[3,4,8,128]{3,2,1,0:T(8,128)} copy(f32[3,4,8,128]{3,2,1,0:T(8,128)S(1)} %get-tuple-element.5) | data formatting | bytes 98304
Async XLA Ops:
  0.6 1.1 %copy-start = (f32[192,768]{1,0:T(8,128)S(1)}, f32[192,768]{1,0:T(8,128)}, u32[]{:S(2)}) copy-start(f32[192,768]{1,0:T(8,128)} %constant.6.clone.z_mat) | copy-start | bytes 1769476
  1.7 1.0 %copy-start.1 = (f32[360,144]{1,0:T(8,128)S(1)}, f32[360,144]{1,0:T(8,128)}, u32[]{:S(2)}) copy-start(f32[360,144]{1,0:T(8,128)} %constant.7.clone.plane_mat) | copy-start | bytes 622084
  2.7 0.9 %copy-start.2 = (f32[256,128]{1,0:T(8,128)S(1)}, f32[256,128]{1,0:T(8,128)}, u32[]{:S(2)}) copy-start(f32[256,128]{1,0:T(8,128)} %constant.8.clone.weave_mat) | copy-start | bytes 393220
  3.6 0.9 %copy-start.3 = (f32[6,12,192]{2,1,0:T(8,128)S(1)}, f32[6,12,192]{2,1,0:T(8,128)}, u32[]{:S(2)}) copy-start(f32[6,12,192]{2,1,0:T(8,128)} %energy.1) | copy-start | bytes 165892
  4.5 0.7 %copy-start.4 = (f32[2,4,64]{2,1,0:T(4,128)S(1)}, f32[2,4,64]{2,1,0:T(4,128)}, u32[]{:S(2)}) copy-start(f32[2,4,64]{2,1,0:T(4,128)} %density.1) | copy-start | bytes 6148
  5.2 0.7 %copy-start.5 = (s32[2,4,64]{2,1,0:T(4,128)S(1)}, s32[2,4,64]{2,1,0:T(4,128)}, u32[]{:S(2)}) copy-start(s32[2,4,64]{2,1,0:T(4,128)} %region.1) | copy-start | bytes 6148
  5.9 0.7 %copy-start.6 = (f32[3]{0:T(128)S(1)}, f32[3]{0:T(128)}, u32[]{:S(2)}) copy-start(f32[3]{0:T(128)} %gamma.1) | copy-start | bytes 40
where the time goes:
time: 29.9 us; the launch traced here: 29.6 us
  Pallas kernels  21.8 us (73%)
  local copies, waits for them, and re-layouts  7.11 us (24%)
  between operations  0.65 us (2%)
    pallas_call x1, Pallas kernels, on_device(): pl.pallas_call(functools.partial(kernel, sizes, cx, cy, cz, lanes), out_s...  21.8 us
    unnamed x16, local copies, waits for them, and re-layouts  7.11 us

commit v1 on v0

--- a/solution.py
+++ b/solution.py
@@ -14,6 +14,9 @@
 WEIGHTS = [5.0 / 18.0, 8.0 / 18.0, 5.0 / 18.0]
 SUB = 8
 PHASES = 3
+LOW, HIGH = 2, 1
+STRIDE = 4
+PACKED = 128 // STRIDE
 
 
 def line_tables():
@@ -38,8 +41,8 @@
     for k in range(3):
         for a in range(3):
             for e in range(cz):
-                out[3 * e + a, k, e] = WEIGHTS[a] * values[a][k]
-                out[3 * e + a, 3 + k, e] = WEIGHTS[a] * slopes[a][k]
+                out[3 * e + a, k, LOW + e] = WEIGHTS[a] * values[a][k]
+                out[3 * e + a, 3 + k, LOW + e] = WEIGHTS[a] * slopes[a][k]
     return out.reshape(3 * cz, 6 * lanes)
 
 
@@ -68,8 +71,8 @@
 def weave_matrix(cz, lanes):
     out = np.zeros((2, lanes, 2 * cz), np.float32)
     for e in range(cz):
-        out[0, e, 2 * e] = 1.0
-        out[1, e, 2 * e + 1] = 1.0
+        out[0, LOW + e, 2 * e] = 1.0
+        out[1, LOW + e, 2 * e + 1] = 1.0
     return out.reshape(2 * lanes, 2 * cz)
 
 
@@ -78,9 +81,11 @@
 
 
 def reduction_stages(sizes):
-    if math.prod(sizes) <= 64:
-        return [(0, 1, 2)]
-    return [(0,), (1,), (2,)]
+    return [(0, 1), (2,)]
+
+
+def message_tiles(cx, cy):
+    return (2 * cx + 1) * (2 * cy + 1) + -(-cx * cy // SUB)
 
 
 def group_size(stage, sizes):
@@ -99,6 +104,14 @@
     if isinstance(step, int):
         return low if step < 0 else high
     return jnp.where(step > 0, high, low)
+
+
+def repeat(size, action):
+    if size <= 8:
+        for offset in range(1, size):
+            action(offset)
+    else:
+        pl.loop(1, size)(action)
 
 
 def under(conditions, action):
@@ -114,18 +127,27 @@
 
 def kernel(
     sizes, cx, cy, cz, lanes,
-    energy, density, region, gamma, z_mat, plane_mat, weave_mat,
+    energy_hbm, density_hbm, region_hbm, gamma_hbm, z_hbm, plane_hbm, weave_hbm,
     acc_out, res_out,
+    energy, density, region, gamma, z_mat, plane_mat, weave_mat, load_sem,
     points, fac, fac_points, dens, part, full, rows, z_part, x_buf, y_buf, xy_buf, z_buf,
-    send_sem, recv_sem, *stage_refs,
+    send_sem, recv_sem, z_send, z_recv, *stage_refs,
 ):
+    loads = [
+        pltpu.make_async_copy(src, dst, load_sem.at[number])
+        for number, (src, dst) in enumerate((
+            (energy_hbm, energy), (density_hbm, density), (region_hbm, region), (gamma_hbm, gamma),
+            (z_hbm, z_mat), (plane_hbm, plane_mat), (weave_hbm, weave_mat),
+        ))
+    ]
+    for load in loads:
+        load.start()
     nx, ny = 2 * cx + 1, 2 * cy + 1
     nodes = nx * ny
     place = [lax.axis_index(name) for name in AXES]
     stages = reduction_stages(sizes)
     centre = (2, 2, 0, None)
     dirs = [axis_directions(place[axis], sizes[axis]) for axis in range(3)]
-    sides = [d + [centre] for d in dirs]
 
     def target(step_x, step_y, step_z):
         return (place[0] + step_x, place[1] + step_y, place[2] + step_z)
@@ -148,11 +170,14 @@
     for stage in stages:
         size = group_size(stage, sizes)
 
-        @pl.loop(1, size)
-        def _(offset, stage=stage):
-            where, _mine = partner(stage, offset)
+        def greet(offset, stage=stage):
+            where, _ = partner(stage, offset)
             pl.semaphore_signal(barrier, inc=1, device_id=where, device_id_type=MESH)
 
+        repeat(size, greet)
+
+    for load in loads[:5]:
+        load.wait()
     for xp in range(3 * cx):
         points[pl.ds(xp * 3 * cy, 3 * cy), :] = energy[xp]
     gamma_elem = jnp.zeros(region.shape, jnp.float32)
@@ -162,8 +187,8 @@
     fac[...] = jnp.zeros_like(fac)
     dens[...] = jnp.zeros_like(dens)
     for i in range(cx):
-        fac[pl.ds(i * cy, cy), pl.ds(0, cz)] = factor[i]
-        dens[pl.ds(i * cy, cy), pl.ds(0, cz)] = density[i]
+        fac[pl.ds(i * cy, cy), pl.ds(LOW, cz)] = factor[i]
+        dens[pl.ds(i * cy, cy), pl.ds(LOW, cz)] = density[i]
     for xp in range(3 * cx):
         for k in range(cy):
             row = fac[pl.ds((xp // 3) * cy + k, 1), :]
@@ -174,6 +199,7 @@
         [scaled[0] + pltpu.roll(scaled[2], 1, 1), scaled[3] + pltpu.roll(scaled[5], 1, 1)], axis=0
     )
     odd = jnp.concatenate([scaled[1], scaled[4]], axis=0)
+    loads[5].wait()
     force = exact_dot(plane_mat[...], jnp.concatenate([even, odd], axis=1))
     sub = lax.broadcasted_iota(jnp.int32, (1, SUB, lanes), 1)
     lane = lax.broadcasted_iota(jnp.int32, (1, SUB, lanes), 2)
@@ -182,30 +208,78 @@
     o_part = force[:, lanes:].reshape(nodes, SUB, lanes)
     part[0] = jnp.where(is_even, e_part, o_part).reshape(ny, nx, SUB, lanes)
 
-    used = jnp.logical_and(lax.rem(sub, 4) < 3, lane < jnp.where(is_even, cz + 1, cz))
-    wall_low = jnp.logical_and(place[2] == 0, jnp.logical_and(is_even, lane == 0))
+    top = LOW + cz
+    used = jnp.logical_and(
+        lax.rem(sub, 4) < 3, lane < jnp.where(is_even, top + HIGH + 1, top + HIGH)
+    )
+    wall_low = jnp.logical_and(place[2] == 0, jnp.logical_and(is_even, lane == LOW))
     wall_high = jnp.logical_and(
-        place[2] == sizes[2] - 1, jnp.logical_and(is_even, lane == cz)
+        place[2] == sizes[2] - 1, jnp.logical_and(is_even, lane == top)
     )
     keep = jnp.where(
         jnp.logical_and(used, jnp.logical_not(jnp.logical_or(wall_low, wall_high))), 1.0, 0.0
     )
-    owned = jnp.where(lane < cz, 1.0, 0.0)
-    ends = [jnp.logical_and(is_even, lane == 0), jnp.logical_and(is_even, lane == cz)]
-    spot = lax.broadcasted_iota(jnp.int32, (nodes, SUB, 128), 0)
-    pack_lane = lax.broadcasted_iota(jnp.int32, (nodes, SUB, 128), 2)
-    pack_hot = jnp.where(spot == pack_lane, 1.0, 0.0)
-    flat_lane = lax.broadcasted_iota(jnp.int32, (SUB, 128), 1)
-    lane_x, lane_y = lax.rem(flat_lane, nx), lax.div(flat_lane, nx)
-
-    def copies(phase, side_x, side_y, side_z):
-        (sx, tx, dx, _), (sy, ty, dy, _), (sz, tz, dz, _) = side_x, side_y, side_z
-        here, there = [phase * 27 + (a * 3 + b) * 3 + c for a, b, c in ((sx, sy, sz), (tx, ty, tz))]
+    owned = jnp.where(jnp.logical_and(lane >= LOW, lane < top), 1.0, 0.0)
+
+    flat_lane = lax.broadcasted_iota(jnp.int32, (SUB, lanes), 1)
+    density_tiles = -(-cx * cy // SUB)
+
+    def tile_of(number):
+        if number < nodes:
+            return part[0, number // nx, number % nx]
+        return dens[pl.ds((number - nodes) * SUB, SUB), :]
+
+    spans = ((LOW, top, HIGH + 1), (top - LOW, 0, LOW + 1))
+
+    def pack_z():
+        for side, (first, _, width) in enumerate(spans):
+            for group in range(-(-(nodes + density_tiles) // PACKED)):
+                tile = jnp.zeros((SUB, lanes), jnp.float32)
+                for number in range(group * PACKED, min((group + 1) * PACKED, nodes + density_tiles)):
+                    at = STRIDE * (number % PACKED)
+                    moved = pltpu.roll(tile_of(number), (at - first) % lanes, 1)
+                    hot = jnp.logical_and(flat_lane >= at, flat_lane < at + width)
+                    tile = tile + jnp.where(hot, moved, 0.0)
+                z_part[side, group] = tile
+
+    def copy_z(side_z, arriving):
+        sz, tz, dz, _ = side_z
+        own, src = z_buf.at[sz], z_part.at[pick(dz, 0, 1)]
+        return pltpu.make_async_remote_copy(
+            src_ref=src, dst_ref=own if arriving else z_buf.at[tz],
+            send_sem=z_send.at[sz], recv_sem=z_recv.at[sz if arriving else tz],
+            device_id=target(0, 0, dz), device_id_type=MESH,
+        )
+
+    def exchange_z():
+        pack_z()
+        for side_z in dirs[2]:
+            under([side_z[3]], lambda side_z=side_z: copy_z(side_z, False).start())
+        for side_z in dirs[2]:
+            under([side_z[3]], lambda side_z=side_z: copy_z(side_z, True).wait_recv())
+        arrived = []
+        for side_z in dirs[2]:
+            sz, _, dz, _ = side_z
+            arrived.append((sz, pick(dz, 0, top), pick(dz, LOW + 1, HIGH + 1)))
+        for number in range(nodes + density_tiles):
+            group, at = divmod(number, PACKED)
+            tile = tile_of(number)
+            for sz, first, width in arrived:
+                shift = first - STRIDE * at
+                shift = shift % lanes if isinstance(shift, int) else lax.rem(shift + lanes, lanes)
+                moved = pltpu.roll(z_buf[sz, group], shift, 1)
+                hot = jnp.logical_and(flat_lane >= first, flat_lane < first + width)
+                tile = tile + jnp.where(hot, moved, 0.0)
+            if number < nodes:
+                part[0, number // nx, number % nx] = tile
+            else:
+                dens[pl.ds((number - nodes) * SUB, SUB), :] = tile
+
+    def copies(phase, side_x, side_y):
+        (sx, tx, dx, _), (sy, ty, dy, _) = side_x, side_y
+        here, there = [phase * 9 + a * 3 + b for a, b in ((sx, sy), (tx, ty))]
         xf, yf = pick(dx, 0, nx - 1), pick(dy, 0, ny - 1)
-        if sz != 2:
-            src = z_part.at[phase, pick(dz, 0, 1)]
-            dst, own = z_buf.at[phase, tz, tx, ty], z_buf.at[phase, sz, sx, sy]
-        elif sy == 2:
+        if sy == 2:
             src = part.at[phase, :, xf]
             dst, own = x_buf.at[phase, tx], x_buf.at[phase, sx]
         elif sx == 2:
@@ -218,21 +292,35 @@
         def make(dst_ref, slot):
             return pltpu.make_async_remote_copy(
                 src_ref=src, dst_ref=dst_ref, send_sem=send_sem.at[here], recv_sem=recv_sem.at[slot],
-                device_id=target(dx, dy, dz), device_id_type=MESH,
+                device_id=target(dx, dy, 0), device_id_type=MESH,
             )
 
         return lambda: make(dst, there), lambda: make(own, here)
 
-    def each(phase, plane, action):
+    def facing(axis, step):
+        chosen = []
+        for direction in dirs[axis]:
+            slot, at, own_step, there = direction
+            if step is None:
+                chosen.append(direction)
+            elif isinstance(own_step, int):
+                if own_step == step:
+                    chosen.append(direction)
+            else:
+                chosen.append((slot, at, step, own_step == step))
+        return chosen + [centre]
+
+    def each(phase, step, action):
+        if phase + 1 < PHASES:
+            step = None
         groups = {}
-        for side_z in [centre] if plane else dirs[2]:
-            for side_x in sides[0]:
-                for side_y in sides[1]:
-                    if side_z[0] == 2 and side_x[0] == 2 and side_y[0] == 2:
-                        continue
-                    conditions = (side_x[3], side_y[3], side_z[3])
-                    key = tuple(None if c is None else s[0] for c, s in zip(conditions, (side_x, side_y, side_z)))
-                    groups.setdefault(key, (conditions, []))[1].append((side_x, side_y, side_z))
+        for side_x in facing(0, step):
+            for side_y in facing(1, step):
+                if side_x[0] == 2 and side_y[0] == 2:
+                    continue
+                conditions = (side_x[3], side_y[3])
+                key = tuple(None if c is None else d[0] for c, d in zip(conditions, (side_x, side_y)))
+                groups.setdefault(key, (conditions, []))[1].append((side_x, side_y))
         for conditions, members in groups.values():
 
             def run(members=members):
@@ -242,46 +330,20 @@
             under(conditions, run)
 
     def start(phase):
-        each(phase, True, lambda pair: pair[0]().start())
-        whole = part[phase].reshape(nodes, SUB, lanes)
-        for side, at in ((0, 0), (1, cz)):
-            z_part[phase, side] = jnp.sum(whole[:, :, at : at + 1] * pack_hot, axis=0)
-        each(phase, False, lambda pair: pair[0]().start())
+        each(phase, 1, lambda pair: pair[0]().start())
 
     def finish(phase):
-        each(phase, True, lambda pair: pair[1]().wait_recv())
-        full[phase] = part[phase]
+        each(phase, -1, lambda pair: pair[1]().wait_recv())
+        full[phase] = part[phase] * keep.reshape(1, 1, SUB, lanes)
         for sx, _, dx, _ in dirs[0]:
             xf = pick(dx, 0, nx - 1)
-            full[phase, :, xf] = full[phase, :, xf] + x_buf[phase, sx]
+            full[phase, :, xf] = full[phase, :, xf] + x_buf[phase, sx] * keep
         for sy, _, dy, _ in dirs[1]:
             yf = pick(dy, 0, ny - 1)
-            full[phase, yf] = full[phase, yf] + y_buf[phase, sy]
+            full[phase, yf] = full[phase, yf] + y_buf[phase, sy] * keep
             for sx, _, dx, _ in dirs[0]:
                 xf = pick(dx, 0, nx - 1)
-                full[phase, yf, xf] = full[phase, yf, xf] + xy_buf[phase, sx, sy]
-        each(phase, False, lambda pair: pair[1]().wait_recv())
-        whole = full[phase].reshape(nodes, SUB, lanes)
-        for sz, _, dz, _ in dirs[2]:
-            tile = z_buf[phase, sz, 2, 2]
-            for sx, _, dx, _ in sides[0]:
-                for sy, _, dy, _ in sides[1]:
-                    if sx == 2 and sy == 2:
-                        continue
-                    moved = pltpu.roll(
-                        z_buf[phase, sz, sx, sy],
-                        lax.rem(dx * (nx - 1) + dy * (ny - 1) * nx + 128, 128), 1,
-                    )
-                    good = flat_lane < nodes
-                    if sx != 2:
-                        good = jnp.logical_and(good, lane_x == pick(dx, 0, nx - 1))
-                    if sy != 2:
-                        good = jnp.logical_and(good, lane_y == pick(dy, 0, ny - 1))
-                    tile = tile + jnp.where(good, moved, 0.0)
-            spread = jnp.sum(tile[None] * pack_hot, axis=2, keepdims=True)
-            end = pick(dz, ends[0], ends[1])
-            whole = whole + jnp.where(end, spread, 0.0)
-        full[phase] = (whole * keep).reshape(ny, nx, SUB, lanes)
+                full[phase, yf, xf] = full[phase, yf, xf] + xy_buf[phase, sx, sy] * keep[0]
         for axis, last in ((0, nx - 1), (1, ny - 1)):
             for at, here in ((0, place[axis] == 0), (last, place[axis] == sizes[axis] - 1)):
 
@@ -364,6 +426,7 @@
 
     if sum(group_size(stage, sizes) - 1 for stage in stages):
         pl.semaphore_wait(barrier, sum(group_size(stage, sizes) - 1 for stage in stages))
+    exchange_z()
     start(0)
     finish(0)
     apply_mass(0, 1)
@@ -378,7 +441,7 @@
         jnp.sum(force_own * force_own, axis=0),
         jnp.sum(force_own * image_own, axis=0),
         jnp.sum(image_own * image_own, axis=0),
-        jnp.sum((full[1] * part[2]).reshape(nodes, SUB, lanes), axis=0),
+        jnp.sum((full[1] * part[2]).reshape(nodes, SUB, lanes) * owned, axis=0),
     ]
     flat_sub = lax.broadcasted_iota(jnp.int32, (SUB, 128), 0)
     message = jnp.zeros((SUB, 128), jnp.float32)
@@ -387,40 +450,37 @@
         message = message + jnp.where(hot, jnp.sum(product, axis=1, keepdims=True), 0.0)
     total = jnp.sum(message, axis=0, keepdims=True)
 
-    woven_force, woven_image = None, None
+    loads[6].wait()
     for number, stage in enumerate(stages):
         slots, stage_send, stage_recv = stage_refs[3 * number : 3 * number + 3]
         size = group_size(stage, sizes)
-        if size == 1:
-            continue
-        _, mine = partner(stage, 0)
-        slots[mine] = total
-
-        @pl.loop(1, size)
-        def _(offset, stage=stage, slots=slots, stage_send=stage_send, stage_recv=stage_recv):
-            where, at = partner(stage, offset)
-            pltpu.make_async_remote_copy(
-                src_ref=slots.at[at], dst_ref=slots.at[at],
-                send_sem=stage_send, recv_sem=stage_recv,
-                device_id=where, device_id_type=MESH,
-            ).start()
-
+        if size > 1:
+            _, mine = partner(stage, 0)
+            slots[mine] = total
+
+            def copy_to(offset, stage=stage, slots=slots, sems=(stage_send, stage_recv)):
+                where, at = partner(stage, offset)
+                pltpu.make_async_remote_copy(
+                    src_ref=slots.at[at], dst_ref=slots.at[at], send_sem=sems[0], recv_sem=sems[1],
+                    device_id=where, device_id_type=MESH,
+                ).start()
+
+            repeat(size, copy_to)
         if number == 0:
             woven_force, woven_image = woven(0), woven(1)
+        elif number == 1:
             finish(2)
-        where, _ = partner(stage, 1)
-        others = slots.at[pl.ds(0, size - 1)]
-        wait = pltpu.make_async_remote_copy(
-            src_ref=others, dst_ref=others, send_sem=stage_send, recv_sem=stage_recv,
-            device_id=where, device_id_type=MESH,
-        )
-        wait.wait_recv()
-        wait.wait_send()
-        total = jnp.sum(slots[...], axis=0)
-    if woven_force is None:
-        woven_force, woven_image = woven(0), woven(1)
-        finish(2)
-    woven_second = woven(2)
+            woven_second = woven(2)
+        if size > 1:
+            where, _ = partner(stage, 1)
+            others = slots.at[pl.ds(0, size - 1)]
+            wait = pltpu.make_async_remote_copy(
+                src_ref=others, dst_ref=others, send_sem=stage_send, recv_sem=stage_recv,
+                device_id=where, device_id_type=MESH,
+            )
+            wait.wait_recv()
+            wait.wait_send()
+            total = jnp.sum(slots[...], axis=0)
 
     row_lane = lax.broadcasted_iota(jnp.int32, (1, 128), 1)
     live = jnp.logical_and(lax.rem(row_lane, 4) == 0, row_lane < 12)
@@ -444,9 +504,10 @@
         acc_out[c] = (a * f - b * q).reshape(2 * cx, 2 * cy, 2 * cz)
         res_out[c] = (f - a * q + b * s).reshape(2 * cx, 2 * cy, 2 * cz)
 
+    for side_z in dirs[2]:
+        under([side_z[3]], lambda side_z=side_z: copy_z(side_z, False).wait_send())
     for phase in range(PHASES):
-        each(phase, True, lambda pair: pair[0]().wait_send())
-        each(phase, False, lambda pair: pair[0]().wait_send())
+        each(phase, 1, lambda pair: pair[0]().wait_send())
 
 
 def solution(mesh):
@@ -454,26 +515,37 @@
 
     def on_device(energy, density, region, gamma_table):
         cx, cy, cz = density.shape
-        lanes = -(-(cz + 1) // 128) * 128
+        lanes = -(-(cz + LOW + HIGH + 1) // 128) * 128
         nx, ny = 2 * cx + 1, 2 * cy + 1
         out = jax.ShapeDtypeStruct((3, 2 * cx, 2 * cy, 2 * cz), jnp.float32)
         vmem = pl.BlockSpec(memory_space=pltpu.VMEM)
+        hbm = pl.BlockSpec(memory_space=pltpu.HBM)
+        tables = [z_matrix(cz, lanes), plane_matrix(cx, cy), weave_matrix(cz, lanes)]
+        groups = -(-message_tiles(cx, cy) // PACKED)
         tile = (SUB, lanes)
         scratch = [
+            pltpu.VMEM(energy.shape, jnp.float32),
+            pltpu.VMEM(density.shape, jnp.float32),
+            pltpu.VMEM(region.shape, jnp.int32),
+            pltpu.SMEM(gamma_table.shape, jnp.float32),
+            *[pltpu.VMEM(table.shape, jnp.float32) for table in tables],
+            pltpu.SemaphoreType.DMA((7,)),
             pltpu.VMEM((9 * cx * cy, 3 * cz), jnp.float32),
             pltpu.VMEM((cx * cy, lanes), jnp.float32),
             pltpu.VMEM((9 * cx * cy, lanes), jnp.float32),
-            pltpu.VMEM((cx * cy, lanes), jnp.float32),
+            pltpu.VMEM((-(-cx * cy // SUB) * SUB, lanes), jnp.float32),
             pltpu.VMEM((PHASES, ny, nx) + tile, jnp.float32),
             pltpu.VMEM((PHASES, ny, nx) + tile, jnp.float32),
             pltpu.VMEM((ny * nx * SUB, lanes), jnp.float32),
-            pltpu.VMEM((PHASES, 2, SUB, 128), jnp.float32),
+            pltpu.VMEM((2, groups) + tile, jnp.float32),
             pltpu.VMEM((PHASES, 2, ny) + tile, jnp.float32),
             pltpu.VMEM((PHASES, 2, nx) + tile, jnp.float32),
             pltpu.VMEM((PHASES, 2, 2) + tile, jnp.float32),
-            pltpu.VMEM((PHASES, 2, 3, 3, SUB, 128), jnp.float32),
-            pltpu.SemaphoreType.DMA((PHASES * 27,)),
-            pltpu.SemaphoreType.DMA((PHASES * 27,)),
+            pltpu.VMEM((2, groups) + tile, jnp.float32),
+            pltpu.SemaphoreType.DMA((PHASES * 9,)),
+            pltpu.SemaphoreType.DMA((PHASES * 9,)),
+            pltpu.SemaphoreType.DMA((2,)),
+            pltpu.SemaphoreType.DMA((2,)),
         ]
         for stage in reduction_stages(sizes):
             scratch += [
@@ -484,17 +556,14 @@
         return pl.pallas_call(
             functools.partial(kernel, sizes, cx, cy, cz, lanes),
             out_shape=(out, out),
-            in_specs=[vmem] * 3 + [pl.BlockSpec(memory_space=pltpu.SMEM)] + [vmem] * 3,
+            in_specs=[hbm] * 7,
             out_specs=(vmem, vmem),
             scratch_shapes=scratch,
             compiler_params=pltpu.CompilerParams(
-                collective_id=0, has_side_effects=True, vmem_limit_bytes=32 * 1024 * 1024
+                collective_id=0, has_side_effects=True, vmem_limit_bytes=60 * 1024 * 1024
             ),
         )(
-            energy, density, region, gamma_table,
-            jnp.asarray(z_matrix(cz, lanes)),
-            jnp.asarray(plane_matrix(cx, cy)),
-            jnp.asarray(weave_matrix(cz, lanes)),
+            energy, density, region, gamma_table, *[jnp.asarray(table) for table in tables],
         )
 
     in_specs = (P(*AXES), P(*AXES), P(*AXES), P())

time: 29.9 us -> 26.5 us (0.89)
  local copies, waits for them, and re-layouts: 7.11 us -> 2.06 us
  Pallas kernels: 21.8 us -> 23.6 us
    unnamed x16 -> x4, local copies, waits for them, and re-layouts: 7.11 us -> 2.06 us
    pallas_call x1, Pallas kernels: 21.8 us -> 23.6 us  [on_device(): pl.pallas_call(functools.partial(kernel, sizes, cx, cy, cz, lanes), out_s...]
where the time goes in v1:
time: 26.5 us; the launch traced here: 26.3 us
  Pallas kernels  23.6 us (89%)
  local copies, waits for them, and re-layouts  2.06 us (8%)
  between operations  0.65 us (2%)
    pallas_call x1, Pallas kernels, on_device(): pl.pallas_call(functools.partial(kernel, sizes, cx, cy, cz, lanes), out_s...  23.6 us
    unnamed x4, local copies, waits for them, and re-layouts  2.06 us

profile of v1, /device:TPU:0, one launch (start us, length us, event | category | flops | bytes accessed | tf_op | source)
XLA Modules:
  0.0 26.3 jit_solution(15400362894856926747)
XLA Ops:
  0.6 23.6 %shard_map.86 = (f32[3,4,8,128]{3,2,1,0:T(8,128)}, f32[3,4,8,128]{3,2,1,0:T(8,128)}) custom-call(f32[6,12,192]{2,1,0:T(8,128)} %energy_hbm.1, f32[2,4,64]{2,1,0:T(4,128)} %density_hbm.1, s32[2,4,64]{2,1,0:T(4,128)} %region_hbm.1, f32[3]{0:T(128)} %gamma_hbm.1, f32[192,768]{1,0:T(8,128)} %constant.6.clone.z_hbm, f32[360,144]{1,0:T(8,128)} %constant.7.clone.plane_hbm, ...), custom_call_target="tpu_custom_call" | custom-call | tf_op jit(solution)/shard_map/pallas_call | solution.py:556
  24.2 0.0 copy-start
  24.2 1.4 %copy.11 = f32[3,4,8,128]{3,2,1,0:T(8,128)} copy(f32[3,4,8,128]{3,2,1,0:T(8,128)} %get-tuple-element.4) | data formatting | bytes 98304
  25.7 0.0 copy-done
  25.7 0.6 %copy.12 = f32[3,4,8,128]{3,2,1,0:T(8,128)} copy(f32[3,4,8,128]{3,2,1,0:T(8,128)S(1)} %copy-done) | data formatting | bytes 98304
Async XLA Ops:
  24.2 1.4 %copy-start = (f32[3,4,8,128]{3,2,1,0:T(8,128)S(1)}, f32[3,4,8,128]{3,2,1,0:T(8,128)}, u32[]{:S(2)}) copy-start(f32[3,4,8,128]{3,2,1,0:T(8,128)} %get-tuple-element.5) | copy-start | bytes 147460

commit v2 on v1

--- a/solution.py
+++ b/solution.py
@@ -60,12 +60,12 @@
     vx, sx = line_matrix(cx, values), line_matrix(cx, slopes)
     vy, sy = line_matrix(cy, values), line_matrix(cy, slopes)
     nx, ny, points = 2 * cx + 1, 2 * cy + 1, 9 * cx * cy
-    out = np.zeros((ny, nx, SUB, 2, points), np.float32)
+    out = np.zeros((ny, nx, SUB, 2, -(-points // 16) * 16), np.float32)
     for c, (mx, my, part) in enumerate(((sx, vy, 0), (vx, sy, 0), (vx, vy, 1))):
         block = np.einsum("xp,yq->yxpq", mx, my).reshape(ny, nx, points)
-        out[:, :, c, part] = block
-        out[:, :, c + 4, part] = block
-    return out.reshape(ny * nx * SUB, 2 * points)
+        out[:, :, c, part, :points] = block
+        out[:, :, c + 4, part, :points] = block
+    return out.reshape(ny * nx * SUB, -1)
 
 
 def weave_matrix(cz, lanes):
@@ -76,12 +76,35 @@
     return out.reshape(2 * lanes, 2 * cz)
 
 
-def exact_dot(a, b):
-    return jnp.dot(a, b, precision=lax.Precision.HIGHEST, preferred_element_type=jnp.float32)
+def halves(array):
+    parts = []
+    rest = array
+    for _ in range(3):
+        piece = rest.astype(jnp.bfloat16)
+        parts.append(piece)
+        rest = rest - piece.astype(jnp.float32)
+    return parts
+
+
+def padded_rows(table):
+    rows = -(-table.shape[0] // 16) * 16
+    return np.pad(table, ((0, rows - table.shape[0]), (0, 0)))
+
+
+def dot(a, b):
+    return jnp.dot(a, b, preferred_element_type=jnp.float32)
+
+
+def by_parts(left, right, count):
+    first = dot(jnp.concatenate(left, axis=0), right[0])
+    second = dot(jnp.concatenate(left[:2], axis=0), right[1])
+    third = dot(left[0], right[2])
+    small = first[2 * count :] + second[count:] + third
+    return first[:count] + (first[count : 2 * count] + second[:count] + small)
 
 
 def reduction_stages(sizes):
-    return [(0, 1), (2,)]
+    return [(0, 1, 2)] if math.prod(sizes) <= 64 else [(0, 1), (2,)]
 
 
 def message_tiles(cx, cy):
@@ -107,7 +130,7 @@
 
 
 def repeat(size, action):
-    if size <= 8:
+    if size <= 64:
         for offset in range(1, size):
             action(offset)
     else:
@@ -154,13 +177,16 @@
 
     def partner(stage, offset):
         mine = 0
+        where = list(place)
         for axis in stage:
             mine = mine * sizes[axis] + place[axis]
-        other = lax.rem(mine + offset, group_size(stage, sizes))
-        where = list(place)
         for axis in reversed(stage):
-            where[axis] = lax.rem(other, sizes[axis])
-            other = lax.div(other, sizes[axis])
+            if isinstance(offset, int):
+                offset, step = divmod(offset, sizes[axis])
+            else:
+                offset, step = lax.div(offset, sizes[axis]), lax.rem(offset, sizes[axis])
+            at = place[axis] + step
+            where[axis] = jnp.where(at >= sizes[axis], at - sizes[axis], at)
         return tuple(where), mine
 
     for ref in (x_buf, y_buf, xy_buf, z_buf):
@@ -178,6 +204,11 @@
 
     for load in loads[:5]:
         load.wait()
+    used_points = 9 * cx * cy
+    if points.shape[0] > used_points:
+        spare = points.shape[0] - used_points
+        points[pl.ds(used_points, spare), :] = jnp.zeros((spare, 3 * cz), jnp.float32)
+        fac_points[pl.ds(used_points, spare), :] = jnp.zeros((spare, lanes), jnp.float32)
     for xp in range(3 * cx):
         points[pl.ds(xp * 3 * cy, 3 * cy), :] = energy[xp]
     gamma_elem = jnp.zeros(region.shape, jnp.float32)
@@ -193,14 +224,19 @@
         for k in range(cy):
             row = fac[pl.ds((xp // 3) * cy + k, 1), :]
             fac_points[pl.ds(xp * 3 * cy + 3 * k, 3), :] = jnp.broadcast_to(row, (3, lanes))
-    sums = exact_dot(points[...], z_mat[...])
+    point_rows = points.shape[0]
+    sums = by_parts(halves(points[...]), halves(z_mat[...]), point_rows)
     scaled = [sums[:, k * lanes : (k + 1) * lanes] * fac_points[...] for k in range(6)]
     even = jnp.concatenate(
         [scaled[0] + pltpu.roll(scaled[2], 1, 1), scaled[3] + pltpu.roll(scaled[5], 1, 1)], axis=0
     )
     odd = jnp.concatenate([scaled[1], scaled[4]], axis=0)
     loads[5].wait()
-    force = exact_dot(plane_mat[...], jnp.concatenate([even, odd], axis=1))
+    force = by_parts(
+        halves(plane_mat[...]),
+        halves(jnp.concatenate([even, odd], axis=1)),
+        plane_mat.shape[0],
+    )[: nodes * SUB]
     sub = lax.broadcasted_iota(jnp.int32, (1, SUB, lanes), 1)
     lane = lax.broadcasted_iota(jnp.int32, (1, SUB, lanes), 2)
     is_even = sub < 4
@@ -242,38 +278,77 @@
                     tile = tile + jnp.where(hot, moved, 0.0)
                 z_part[side, group] = tile
 
-    def copy_z(side_z, arriving):
-        sz, tz, dz, _ = side_z
-        own, src = z_buf.at[sz], z_part.at[pick(dz, 0, 1)]
+    def copy_z(side_z, side_x, side_y, arriving):
+        (sx, tx, dx, _), (sy, ty, dy, _), (sz, tz, dz, _) = side_x, side_y, side_z
+        here, there = [(c * 3 + a) * 3 + b for a, b, c in ((sx, sy, sz), (tx, ty, tz))]
         return pltpu.make_async_remote_copy(
-            src_ref=src, dst_ref=own if arriving else z_buf.at[tz],
-            send_sem=z_send.at[sz], recv_sem=z_recv.at[sz if arriving else tz],
-            device_id=target(0, 0, dz), device_id_type=MESH,
+            src_ref=z_part.at[pick(dz, 0, 1)],
+            dst_ref=z_buf.at[sz, sx, sy] if arriving else z_buf.at[tz, tx, ty],
+            send_sem=z_send.at[here], recv_sem=z_recv.at[here if arriving else there],
+            device_id=target(dx, dy, dz), device_id_type=MESH,
         )
 
-    def exchange_z():
-        pack_z()
+    def each_z(action):
         for side_z in dirs[2]:
-            under([side_z[3]], lambda side_z=side_z: copy_z(side_z, False).start())
-        for side_z in dirs[2]:
-            under([side_z[3]], lambda side_z=side_z: copy_z(side_z, True).wait_recv())
-        arrived = []
-        for side_z in dirs[2]:
-            sz, _, dz, _ = side_z
-            arrived.append((sz, pick(dz, 0, top), pick(dz, LOW + 1, HIGH + 1)))
+            for side_x in dirs[0] + [centre]:
+                ys = dirs[1] + [centre]
+                free = [side_y for side_y in ys if side_y[3] is None]
+
+                def run(side_z=side_z, side_x=side_x, free=free):
+                    for side_y in free:
+                        action(side_z, side_x, side_y)
+
+                under([side_z[3], side_x[3]], run)
+                for side_y in ys:
+                    if side_y[3] is not None:
+                        under(
+                            [side_z[3], side_x[3], side_y[3]],
+                            lambda a=side_z, b=side_x, c=side_y: action(a, b, c),
+                        )
+
+    def piece_z(side_z, sx, sy, number):
+        sz, _, dz, _ = side_z
+        first, width = pick(dz, 0, top), pick(dz, LOW + 1, HIGH + 1)
+        if isinstance(number, int):
+            group, at = divmod(number, PACKED)
+        else:
+            group, at = lax.div(number, PACKED), lax.rem(number, PACKED)
+        shift = first - STRIDE * at
+        shift = shift % lanes if isinstance(shift, int) else lax.rem(shift + lanes, lanes)
+        moved = pltpu.roll(z_buf[sz, sx, sy, group], shift, 1)
+        return jnp.where(jnp.logical_and(flat_lane >= first, flat_lane < first + width), moved, 0.0)
+
+    def add_z():
+        each_z(lambda a, b, c: copy_z(a, b, c, True).wait_recv())
         for number in range(nodes + density_tiles):
-            group, at = divmod(number, PACKED)
-            tile = tile_of(number)
-            for sz, first, width in arrived:
-                shift = first - STRIDE * at
-                shift = shift % lanes if isinstance(shift, int) else lax.rem(shift + lanes, lanes)
-                moved = pltpu.roll(z_buf[sz, group], shift, 1)
-                hot = jnp.logical_and(flat_lane >= first, flat_lane < first + width)
-                tile = tile + jnp.where(hot, moved, 0.0)
             if number < nodes:
-                part[0, number // nx, number % nx] = tile
+                tile = full[0, number // nx, number % nx]
+            else:
+                tile = dens[pl.ds((number - nodes) * SUB, SUB), :]
+            for side_z in dirs[2]:
+                tile = tile + piece_z(side_z, 2, 2, number)
+            if number < nodes:
+                full[0, number // nx, number % nx] = tile
             else:
                 dens[pl.ds((number - nodes) * SUB, SUB), :] = tile
+        for side_x in dirs[0]:
+            xf, from_x = pick(side_x[2], 0, nx - 1), pick(side_x[2], nx - 1, 0)
+            for y in range(ny):
+                full[0, y, xf] = full[0, y, xf] + sum(
+                    piece_z(side_z, side_x[0], 2, y * nx + from_x) for side_z in dirs[2]
+                )
+        for side_y in dirs[1]:
+            yf, from_y = pick(side_y[2], 0, ny - 1), pick(side_y[2], ny - 1, 0)
+            for x in range(nx):
+                full[0, yf, x] = full[0, yf, x] + sum(
+                    piece_z(side_z, 2, side_y[0], from_y * nx + x) for side_z in dirs[2]
+                )
+            for side_x in dirs[0]:
+                xf, from_x = pick(side_x[2], 0, nx - 1), pick(side_x[2], nx - 1, 0)
+                full[0, yf, xf] = full[0, yf, xf] + sum(
+                    piece_z(side_z, side_x[0], side_y[0], from_y * nx + from_x)
+                    for side_z in dirs[2]
+                )
 
     def copies(phase, side_x, side_y):
         (sx, tx, dx, _), (sy, ty, dy, _) = side_x, side_y
@@ -334,16 +409,19 @@
 
     def finish(phase):
         each(phase, -1, lambda pair: pair[1]().wait_recv())
-        full[phase] = part[phase] * keep.reshape(1, 1, SUB, lanes)
+        full[phase] = part[phase]
         for sx, _, dx, _ in dirs[0]:
             xf = pick(dx, 0, nx - 1)
-            full[phase, :, xf] = full[phase, :, xf] + x_buf[phase, sx] * keep
+            full[phase, :, xf] = full[phase, :, xf] + x_buf[phase, sx]
         for sy, _, dy, _ in dirs[1]:
             yf = pick(dy, 0, ny - 1)
-            full[phase, yf] = full[phase, yf] + y_buf[phase, sy] * keep
+            full[phase, yf] = full[phase, yf] + y_buf[phase, sy]
             for sx, _, dx, _ in dirs[0]:
                 xf = pick(dx, 0, nx - 1)
-                full[phase, yf, xf] = full[phase, yf, xf] + xy_buf[phase, sx, sy] * keep[0]
+                full[phase, yf, xf] = full[phase, yf, xf] + xy_buf[phase, sx, sy]
+        if phase == 0 and dirs[2]:
+            add_z()
+        full[phase] = full[phase] * keep.reshape(1, 1, SUB, lanes)
         for axis, last in ((0, nx - 1), (1, ny - 1)):
             for at, here in ((0, place[axis] == 0), (last, place[axis] == sizes[axis] - 1)):
 
@@ -412,9 +490,9 @@
 
     def woven(phase):
         rows[...] = full[phase].reshape(nodes * SUB, lanes)
-        halves = []
+        sides = []
         for first in (0, 4):
-            halves.append(jnp.concatenate(
+            sides.append(jnp.concatenate(
                 [
                     rows[pl.ds(x * SUB + first + c, 2 * cy, stride=nx * SUB), :]
                     for c in range(3)
@@ -422,17 +500,28 @@
                 ],
                 axis=0,
             ))
-        return exact_dot(jnp.concatenate(halves, axis=1), weave_mat[...])
+        wide = jnp.concatenate(sides, axis=1)
+        count = wide.shape[0]
+        out = dot(jnp.concatenate(halves(wide), axis=0), weave_mat[...].astype(jnp.bfloat16))
+        return out[:count] + (out[count : 2 * count] + out[2 * count :])
 
     if sum(group_size(stage, sizes) - 1 for stage in stages):
         pl.semaphore_wait(barrier, sum(group_size(stage, sizes) - 1 for stage in stages))
-    exchange_z()
     start(0)
+    if dirs[2]:
+        pack_z()
+        each_z(lambda a, b, c: copy_z(a, b, c, False).start())
     finish(0)
-    apply_mass(0, 1)
-    start(1)
-    finish(1)
-    apply_mass(1, 2)
+
+    @pl.loop(0, PHASES - 1)
+    def _(number):
+        apply_mass(number, number + 1)
+
+        @pl.when(number == 0)
+        def _():
+            start(1)
+            finish(1)
+
     start(2)
 
     force_own = full[0, : ny - 1, : nx - 1].reshape(4 * cx * cy, SUB, lanes) * owned
@@ -468,7 +557,6 @@
             repeat(size, copy_to)
         if number == 0:
             woven_force, woven_image = woven(0), woven(1)
-        elif number == 1:
             finish(2)
             woven_second = woven(2)
         if size > 1:
@@ -504,8 +592,7 @@
         acc_out[c] = (a * f - b * q).reshape(2 * cx, 2 * cy, 2 * cz)
         res_out[c] = (f - a * q + b * s).reshape(2 * cx, 2 * cy, 2 * cz)
 
-    for side_z in dirs[2]:
-        under([side_z[3]], lambda side_z=side_z: copy_z(side_z, False).wait_send())
+    each_z(lambda a, b, c: copy_z(a, b, c, False).wait_send())
     for phase in range(PHASES):
         each(phase, 1, lambda pair: pair[0]().wait_send())
 
@@ -520,7 +607,12 @@
         out = jax.ShapeDtypeStruct((3, 2 * cx, 2 * cy, 2 * cz), jnp.float32)
         vmem = pl.BlockSpec(memory_space=pltpu.VMEM)
         hbm = pl.BlockSpec(memory_space=pltpu.HBM)
-        tables = [z_matrix(cz, lanes), plane_matrix(cx, cy), weave_matrix(cz, lanes)]
+        tables = [
+            padded_rows(z_matrix(cz, lanes)),
+            padded_rows(plane_matrix(cx, cy)),
+            weave_matrix(cz, lanes),
+        ]
+        assert 3 * cz % 16 == 0
         groups = -(-message_tiles(cx, cy) // PACKED)
         tile = (SUB, lanes)
         scratch = [
@@ -530,9 +622,9 @@
             pltpu.SMEM(gamma_table.shape, jnp.float32),
             *[pltpu.VMEM(table.shape, jnp.float32) for table in tables],
             pltpu.SemaphoreType.DMA((7,)),
-            pltpu.VMEM((9 * cx * cy, 3 * cz), jnp.float32),
+            pltpu.VMEM((-(-9 * cx * cy // 16) * 16, 3 * cz), jnp.float32),
             pltpu.VMEM((cx * cy, lanes), jnp.float32),
-            pltpu.VMEM((9 * cx * cy, lanes), jnp.float32),
+            pltpu.VMEM((-(-9 * cx * cy // 16) * 16, lanes), jnp.float32),
             pltpu.VMEM((-(-cx * cy // SUB) * SUB, lanes), jnp.float32),
             pltpu.VMEM((PHASES, ny, nx) + tile, jnp.float32),
             pltpu.VMEM((PHASES, ny, nx) + tile, jnp.float32),
@@ -541,11 +633,11 @@
             pltpu.VMEM((PHASES, 2, ny) + tile, jnp.float32),
             pltpu.VMEM((PHASES, 2, nx) + tile, jnp.float32),
             pltpu.VMEM((PHASES, 2, 2) + tile, jnp.float32),
-            pltpu.VMEM((2, groups) + tile, jnp.float32),
+            pltpu.VMEM((2, 3, 3, groups) + tile, jnp.float32),
             pltpu.SemaphoreType.DMA((PHASES * 9,)),
             pltpu.SemaphoreType.DMA((PHASES * 9,)),
-            pltpu.SemaphoreType.DMA((2,)),
-            pltpu.SemaphoreType.DMA((2,)),
+            pltpu.SemaphoreType.DMA((18,)),
+            pltpu.SemaphoreType.DMA((18,)),
         ]
         for stage in reduction_stages(sizes):
             scratch += [

time: 26.5 us -> 22.7 us (0.86)
  Pallas kernels: 23.6 us -> 19.8 us
    pallas_call x1, Pallas kernels: 23.6 us -> 19.8 us  [on_device(): pl.pallas_call(functools.partial(kernel, sizes, cx, cy, cz, lanes), out_s...]
where the time goes in v2:
time: 22.7 us; the launch traced here: 22.5 us
  Pallas kernels  19.8 us (87%)
  local copies, waits for them, and re-layouts  2.06 us (9%)
  between operations  0.65 us (3%)
    pallas_call x1, Pallas kernels, on_device(): pl.pallas_call(functools.partial(kernel, sizes, cx, cy, cz, lanes), out_s...  19.8 us
    unnamed x4, local copies, waits for them, and re-layouts  2.06 us

profile of v2, /device:TPU:0, one launch (start us, length us, event | category | flops | bytes accessed | tf_op | source)
XLA Modules:
  0.0 22.5 jit_solution(10311166581127109512)
XLA Ops:
  0.6 19.8 %shard_map.86 = (f32[3,4,8,128]{3,2,1,0:T(8,128)}, f32[3,4,8,128]{3,2,1,0:T(8,128)}) custom-call(f32[6,12,192]{2,1,0:T(8,128)} %energy_hbm.1, f32[2,4,64]{2,1,0:T(4,128)} %density_hbm.1, s32[2,4,64]{2,1,0:T(4,128)} %region_hbm.1, f32[3]{0:T(128)} %gamma_hbm.1, f32[192,768]{1,0:T(8,128)} %constant.6.clone.z_hbm, f32[368,160]{1,0:T(8,128)} %constant.7.clone.plane_hbm, ...), custom_call_target="tpu_custom_call" | custom-call | tf_op jit(solution)/shard_map/pallas_call | solution.py:648
  20.4 0.0 copy-start
  20.5 1.4 %copy.11 = f32[3,4,8,128]{3,2,1,0:T(8,128)} copy(f32[3,4,8,128]{3,2,1,0:T(8,128)} %get-tuple-element.4) | data formatting | bytes 98304
  21.9 0.0 copy-done
  21.9 0.6 %copy.12 = f32[3,4,8,128]{3,2,1,0:T(8,128)} copy(f32[3,4,8,128]{3,2,1,0:T(8,128)S(1)} %copy-done) | data formatting | bytes 98304
Async XLA Ops:
  20.4 1.4 %copy-start = (f32[3,4,8,128]{3,2,1,0:T(8,128)S(1)}, f32[3,4,8,128]{3,2,1,0:T(8,128)}, u32[]{:S(2)}) copy-start(f32[3,4,8,128]{3,2,1,0:T(8,128)} %get-tuple-element.5) | copy-start | bytes 147460

commit v3 on v2

--- a/solution.py
+++ b/solution.py
@@ -33,17 +33,6 @@
 def line_mass():
     values, _ = line_tables()
     return values.T @ np.diag(WEIGHTS) @ values
-
-
-def z_matrix(cz, lanes):
-    values, slopes = line_tables()
-    out = np.zeros((3 * cz, 6, lanes), np.float32)
-    for k in range(3):
-        for a in range(3):
-            for e in range(cz):
-                out[3 * e + a, k, LOW + e] = WEIGHTS[a] * values[a][k]
-                out[3 * e + a, 3 + k, LOW + e] = WEIGHTS[a] * slopes[a][k]
-    return out.reshape(3 * cz, 6 * lanes)
 
 
 def line_matrix(count, table):
@@ -68,12 +57,24 @@
     return out.reshape(ny * nx * SUB, -1)
 
 
-def weave_matrix(cz, lanes):
-    out = np.zeros((2, lanes, 2 * cz), np.float32)
-    for e in range(cz):
-        out[0, LOW + e, 2 * e] = 1.0
-        out[1, LOW + e, 2 * e + 1] = 1.0
-    return out.reshape(2 * lanes, 2 * cz)
+def iota(shape, dim):
+    return lax.broadcasted_iota(jnp.int32, shape, dim)
+
+
+def ones_where(condition):
+    return jnp.where(condition, 1.0, 0.0).astype(jnp.bfloat16)
+
+
+def points_to_elements(cz, lanes):
+    shape = (3 * cz, lanes)
+    offset = iota(shape, 0) - 3 * (iota(shape, 1) - LOW)
+    return jnp.concatenate([ones_where(offset == a) for a in range(3)], axis=1)
+
+
+def elements_to_nodes(cz, lanes):
+    shape = (lanes, 2 * cz)
+    offset = iota(shape, 1) - 2 * (iota(shape, 0) - LOW)
+    return jnp.concatenate([ones_where(offset == a) for a in range(2)], axis=0)
 
 
 def halves(array):
@@ -93,6 +94,12 @@
 
 def dot(a, b):
     return jnp.dot(a, b, preferred_element_type=jnp.float32)
+
+
+def placed(array, table):
+    count = array.shape[0]
+    out = dot(jnp.concatenate(halves(array), axis=0), table)
+    return out[:count] + (out[count : 2 * count] + out[2 * count :])
 
 
 def by_parts(left, right, count):
@@ -150,9 +157,9 @@
 
 def kernel(
     sizes, cx, cy, cz, lanes,
-    energy_hbm, density_hbm, region_hbm, gamma_hbm, z_hbm, plane_hbm, weave_hbm,
-    acc_out, res_out,
-    energy, density, region, gamma, z_mat, plane_mat, weave_mat, load_sem,
+    energy_hbm, density_hbm, region_hbm, gamma_hbm, plane_hbm,
+    out,
+    energy, density, region, gamma, plane_mat, load_sem,
     points, fac, fac_points, dens, part, full, rows, z_part, x_buf, y_buf, xy_buf, z_buf,
     send_sem, recv_sem, z_send, z_recv, *stage_refs,
 ):
@@ -160,7 +167,7 @@
         pltpu.make_async_copy(src, dst, load_sem.at[number])
         for number, (src, dst) in enumerate((
             (energy_hbm, energy), (density_hbm, density), (region_hbm, region), (gamma_hbm, gamma),
-            (z_hbm, z_mat), (plane_hbm, plane_mat), (weave_hbm, weave_mat),
+            (plane_hbm, plane_mat),
         ))
     ]
     for load in loads:
@@ -202,7 +209,7 @@
 
         repeat(size, greet)
 
-    for load in loads[:5]:
+    for load in loads[:4]:
         load.wait()
     used_points = 9 * cx * cy
     if points.shape[0] > used_points:
@@ -224,14 +231,18 @@
         for k in range(cy):
             row = fac[pl.ds((xp // 3) * cy + k, 1), :]
             fac_points[pl.ds(xp * 3 * cy + 3 * k, 3), :] = jnp.broadcast_to(row, (3, lanes))
-    point_rows = points.shape[0]
-    sums = by_parts(halves(points[...]), halves(z_mat[...]), point_rows)
-    scaled = [sums[:, k * lanes : (k + 1) * lanes] * fac_points[...] for k in range(6)]
+    values, slopes = line_tables()
+    spread = placed(points[...], points_to_elements(cz, lanes))
+    scaled = [spread[:, a * lanes : (a + 1) * lanes] * fac_points[...] for a in range(3)]
+
+    def node_sums(table, k):
+        return sum(float(WEIGHTS[a] * table[a][k]) * scaled[a] for a in range(3))
+
     even = jnp.concatenate(
-        [scaled[0] + pltpu.roll(scaled[2], 1, 1), scaled[3] + pltpu.roll(scaled[5], 1, 1)], axis=0
+        [node_sums(t, 0) + pltpu.roll(node_sums(t, 2), 1, 1) for t in (values, slopes)], axis=0
     )
-    odd = jnp.concatenate([scaled[1], scaled[4]], axis=0)
-    loads[5].wait()
+    odd = jnp.concatenate([node_sums(t, 1) for t in (values, slopes)], axis=0)
+    loads[4].wait()
     force = by_parts(
         halves(plane_mat[...]),
         halves(jnp.concatenate([even, odd], axis=1)),
@@ -500,10 +511,7 @@
                 ],
                 axis=0,
             ))
-        wide = jnp.concatenate(sides, axis=1)
-        count = wide.shape[0]
-        out = dot(jnp.concatenate(halves(wide), axis=0), weave_mat[...].astype(jnp.bfloat16))
-        return out[:count] + (out[count : 2 * count] + out[2 * count :])
+        return placed(jnp.concatenate(sides, axis=1), weave)
 
     if sum(group_size(stage, sizes) - 1 for stage in stages):
         pl.semaphore_wait(barrier, sum(group_size(stage, sizes) - 1 for stage in stages))
@@ -539,7 +547,7 @@
         message = message + jnp.where(hot, jnp.sum(product, axis=1, keepdims=True), 0.0)
     total = jnp.sum(message, axis=0, keepdims=True)
 
-    loads[6].wait()
+    weave = elements_to_nodes(cz, lanes)
     for number, stage in enumerate(stages):
         slots, stage_send, stage_recv = stage_refs[3 * number : 3 * number + 3]
         size = group_size(stage, sizes)
@@ -589,8 +597,8 @@
         b = jnp.sum(jnp.where(hot, inner, 0.0), axis=1, keepdims=True)
         here = slice(c * per, (c + 1) * per)
         f, q, s = woven_force[here], woven_image[here], woven_second[here]
-        acc_out[c] = (a * f - b * q).reshape(2 * cx, 2 * cy, 2 * cz)
-        res_out[c] = (f - a * q + b * s).reshape(2 * cx, 2 * cy, 2 * cz)
+        out[0, c] = (a * f - b * q).reshape(2 * cx, 2 * cy, 2 * cz)
+        out[1, c] = (f - a * q + b * s).reshape(2 * cx, 2 * cy, 2 * cz)
 
     each_z(lambda a, b, c: copy_z(a, b, c, False).wait_send())
     for phase in range(PHASES):
@@ -604,15 +612,11 @@
         cx, cy, cz = density.shape
         lanes = -(-(cz + LOW + HIGH + 1) // 128) * 128
         nx, ny = 2 * cx + 1, 2 * cy + 1
-        out = jax.ShapeDtypeStruct((3, 2 * cx, 2 * cy, 2 * cz), jnp.float32)
+        out = jax.ShapeDtypeStruct((2, 3, 2 * cx, 2 * cy, 2 * cz), jnp.float32)
         vmem = pl.BlockSpec(memory_space=pltpu.VMEM)
         hbm = pl.BlockSpec(memory_space=pltpu.HBM)
-        tables = [
-            padded_rows(z_matrix(cz, lanes)),
-            padded_rows(plane_matrix(cx, cy)),
-            weave_matrix(cz, lanes),
-        ]
-        assert 3 * cz % 16 == 0
+        plane = padded_rows(plane_matrix(cx, cy))
+        assert 3 * cz % 16 == 0 and lanes % 16 == 0
         groups = -(-message_tiles(cx, cy) // PACKED)
         tile = (SUB, lanes)
         scratch = [
@@ -620,8 +624,8 @@
             pltpu.VMEM(density.shape, jnp.float32),
             pltpu.VMEM(region.shape, jnp.int32),
             pltpu.SMEM(gamma_table.shape, jnp.float32),
-            *[pltpu.VMEM(table.shape, jnp.float32) for table in tables],
-            pltpu.SemaphoreType.DMA((7,)),
+            pltpu.VMEM(plane.shape, jnp.float32),
+            pltpu.SemaphoreType.DMA((5,)),
             pltpu.VMEM((-(-9 * cx * cy // 16) * 16, 3 * cz), jnp.float32),
             pltpu.VMEM((cx * cy, lanes), jnp.float32),
             pltpu.VMEM((-(-9 * cx * cy // 16) * 16, lanes), jnp.float32),
@@ -645,18 +649,19 @@
                 pltpu.SemaphoreType.DMA,
                 pltpu.SemaphoreType.DMA,
             ]
-        return pl.pallas_call(
+        both = pl.pallas_call(
             functools.partial(kernel, sizes, cx, cy, cz, lanes),
-            out_shape=(out, out),
-            in_specs=[hbm] * 7,
-            out_specs=(vmem, vmem),
+            out_shape=out,
+            in_specs=[hbm] * 5,
+            out_specs=vmem,
             scratch_shapes=scratch,
             compiler_params=pltpu.CompilerParams(
                 collective_id=0, has_side_effects=True, vmem_limit_bytes=60 * 1024 * 1024
             ),
         )(
-            energy, density, region, gamma_table, *[jnp.asarray(table) for table in tables],
+            energy, density, region, gamma_table, jnp.asarray(plane),
         )
+        return both[0], both[1]
 
     in_specs = (P(*AXES), P(*AXES), P(*AXES), P())
     out_specs = (P(None, *AXES), P(None, *AXES))

time: 22.7 us -> 21.8 us (0.960)
  local copies, waits for them, and re-layouts: 2.06 us -> 1.46 us
  Pallas kernels: 19.8 us -> 19.5 us
    unnamed x4 -> x0, local copies, waits for them, and re-layouts: 2.06 us -> none
    squeeze x0 -> x1, local copies, waits for them, and re-layouts: none -> 1.46 us  [on_device(): return (both[0], both[1])]
    pallas_call x1, Pallas kernels: 19.8 us -> 19.5 us  [on_device(): pl.pallas_call(functools.partial(kernel, sizes, cx, cy, cz, lanes), out_s...]
where the time goes in v3:
time: 21.8 us; the launch traced here: 21.6 us
  Pallas kernels  19.5 us (89%)
  local copies, waits for them, and re-layouts  1.46 us (7%)
  between operations  0.64 us (3%)
    pallas_call x1, Pallas kernels, on_device(): pl.pallas_call(functools.partial(kernel, sizes, cx, cy, cz, lanes), out_s...  19.5 us
    squeeze x1, local copies, waits for them, and re-layouts, on_device(): return (both[0], both[1])  1.46 us

profile of v3, /device:TPU:0, one launch (start us, length us, event | category | flops | bytes accessed | tf_op | source)
XLA Modules:
  0.0 21.6 jit_solution(10110584538554729936)
XLA Ops:
  0.6 19.5 %shard_map.68 = f32[2,3,4,8,128]{4,3,2,1,0:T(8,128)} custom-call(f32[6,12,192]{2,1,0:T(8,128)} %energy_hbm.1, f32[2,4,64]{2,1,0:T(4,128)} %density_hbm.1, s32[2,4,64]{2,1,0:T(4,128)} %region_hbm.1, f32[3]{0:T(128)} %gamma_hbm.1, f32[368,160]{1,0:T(8,128)} %constant.2.clone.plane_hbm), custom_call_target="tpu_custom_call" | custom-call | tf_op jit(solution)/shard_map/pallas_call | solution.py:652
  20.2 1.5 %slice_bitcast_fusion = (f32[3,4,8,128]{3,2,1,0:T(8,128)}, f32[3,4,8,128]{3,2,1,0:T(8,128)}) fusion(f32[2,3,4,8,128]{4,3,2,1,0:T(8,128)} %shard_map.68), kind=kLoop, calls=%fused_computation | loop fusion | bytes 196608 | tf_op jit(solution)/shard_map/squeeze | solution.py:664

commit v4 on v3

--- a/solution.py
+++ b/solution.py
@@ -111,7 +111,7 @@
 
 
 def reduction_stages(sizes):
-    return [(0, 1, 2)] if math.prod(sizes) <= 64 else [(0, 1), (2,)]
+    return [(0, 1), (2,)]
 
 
 def message_tiles(cx, cy):
@@ -196,6 +196,24 @@
             where[axis] = jnp.where(at >= sizes[axis], at - sizes[axis], at)
         return tuple(where), mine
 
+    def each_z(action):
+        for side_z in dirs[2]:
+            for side_x in dirs[0] + [centre]:
+                ys = dirs[1] + [centre]
+                free = [side_y for side_y in ys if side_y[3] is None]
+
+                def run(side_z=side_z, side_x=side_x, free=free):
+                    for side_y in free:
+                        action(side_z, side_x, side_y)
+
+                under([side_z[3], side_x[3]], run)
+                for side_y in ys:
+                    if side_y[3] is not None:
+                        under(
+                            [side_z[3], side_x[3], side_y[3]],
+                            lambda a=side_z, b=side_x, c=side_y: action(a, b, c),
+                        )
+
     for ref in (x_buf, y_buf, xy_buf, z_buf):
         ref[...] = jnp.zeros_like(ref)
 
@@ -208,6 +226,15 @@
             pl.semaphore_signal(barrier, inc=1, device_id=where, device_id_type=MESH)
 
         repeat(size, greet)
+
+    def greet_across(side_z, side_x, side_y):
+        if side_x[0] != 2 or side_y[0] != 2:
+            pl.semaphore_signal(
+                barrier, inc=1, device_id=target(side_x[2], side_y[2], side_z[2]),
+                device_id_type=MESH,
+            )
+
+    each_z(greet_across)
 
     for load in loads[:4]:
         load.wait()
@@ -298,24 +325,6 @@
             send_sem=z_send.at[here], recv_sem=z_recv.at[here if arriving else there],
             device_id=target(dx, dy, dz), device_id_type=MESH,
         )
-
-    def each_z(action):
-        for side_z in dirs[2]:
-            for side_x in dirs[0] + [centre]:
-                ys = dirs[1] + [centre]
-                free = [side_y for side_y in ys if side_y[3] is None]
-
-                def run(side_z=side_z, side_x=side_x, free=free):
-                    for side_y in free:
-                        action(side_z, side_x, side_y)
-
-                under([side_z[3], side_x[3]], run)
-                for side_y in ys:
-                    if side_y[3] is not None:
-                        under(
-                            [side_z[3], side_x[3], side_y[3]],
-                            lambda a=side_z, b=side_x, c=side_y: action(a, b, c),
-                        )
 
     def piece_z(side_z, sx, sy, number):
         sz, _, dz, _ = side_z
@@ -513,8 +522,13 @@
             ))
         return placed(jnp.concatenate(sides, axis=1), weave)
 
-    if sum(group_size(stage, sizes) - 1 for stage in stages):
-        pl.semaphore_wait(barrier, sum(group_size(stage, sizes) - 1 for stage in stages))
+    def present(axis):
+        there = [1 if d[3] is None else jnp.where(d[3], 1, 0) for d in dirs[axis]]
+        return sum(there) if there else 0
+
+    around = (1 + present(0)) * (1 + present(1)) - 1
+    in_stages = sum(group_size(stage, sizes) - 1 for stage in stages)
+    pl.semaphore_wait(barrier, in_stages + present(2) * around)
     start(0)
     if dirs[2]:
         pack_z()
@@ -565,6 +579,7 @@
             repeat(size, copy_to)
         if number == 0:
             woven_force, woven_image = woven(0), woven(1)
+        elif number == 1:
             finish(2)
             woven_second = woven(2)
         if size > 1:

time: 21.8 us -> 23.7 us (1.087)
  Pallas kernels: 19.5 us -> 21.4 us
    pallas_call x1, Pallas kernels: 19.5 us -> 21.4 us  [on_device(): pl.pallas_call(functools.partial(kernel, sizes, cx, cy, cz, lanes), out_s...]
where the time goes in v4:
time: 23.7 us; the launch traced here: 23.5 us
  Pallas kernels  21.4 us (90%)
  local copies, waits for them, and re-layouts  1.46 us (6%)
  between operations  0.64 us (3%)
    pallas_call x1, Pallas kernels, on_device(): pl.pallas_call(functools.partial(kernel, sizes, cx, cy, cz, lanes), out_s...  21.4 us
    squeeze x1, local copies, waits for them, and re-layouts, on_device(): return (both[0], both[1])  1.46 us

profile of v4, /device:TPU:0, one launch (start us, length us, event | category | flops | bytes accessed | tf_op | source)
XLA Modules:
  0.0 23.5 jit_solution(12104958839670987612)
XLA Ops:
  0.6 21.4 %shard_map.68 = f32[2,3,4,8,128]{4,3,2,1,0:T(8,128)} custom-call(f32[6,12,192]{2,1,0:T(8,128)} %energy_hbm.1, f32[2,4,64]{2,1,0:T(4,128)} %density_hbm.1, s32[2,4,64]{2,1,0:T(4,128)} %region_hbm.1, f32[3]{0:T(128)} %gamma_hbm.1, f32[368,160]{1,0:T(8,128)} %constant.2.clone.plane_hbm), custom_call_target="tpu_custom_call" | custom-call | tf_op jit(solution)/shard_map/pallas_call | solution.py:667
  22.0 1.5 %slice_bitcast_fusion = (f32[3,4,8,128]{3,2,1,0:T(8,128)}, f32[3,4,8,128]{3,2,1,0:T(8,128)}) fusion(f32[2,3,4,8,128]{4,3,2,1,0:T(8,128)} %shard_map.68), kind=kLoop, calls=%fused_computation | loop fusion | bytes 196608 | tf_op jit(solution)/shard_map/squeeze | solution.py:679

commit v5 on v3

--- a/solution.py
+++ b/solution.py
@@ -567,6 +567,9 @@
             woven_force, woven_image = woven(0), woven(1)
             finish(2)
             woven_second = woven(2)
+            each_z(lambda a, b, c: copy_z(a, b, c, False).wait_send())
+            for phase in range(PHASES):
+                each(phase, 1, lambda pair: pair[0]().wait_send())
         if size > 1:
             where, _ = partner(stage, 1)
             others = slots.at[pl.ds(0, size - 1)]
@@ -599,10 +602,6 @@
         f, q, s = woven_force[here], woven_image[here], woven_second[here]
         out[0, c] = (a * f - b * q).reshape(2 * cx, 2 * cy, 2 * cz)
         out[1, c] = (f - a * q + b * s).reshape(2 * cx, 2 * cy, 2 * cz)
-
-    each_z(lambda a, b, c: copy_z(a, b, c, False).wait_send())
-    for phase in range(PHASES):
-        each(phase, 1, lambda pair: pair[0]().wait_send())
 
 
 def solution(mesh):

time: 21.8 us -> 21.8 us (level)
  no operation moved by 1% of the time
where the time goes in v5:
time: 21.8 us; the launch traced here: 21.6 us
  Pallas kernels  19.5 us (89%)
  local copies, waits for them, and re-layouts  1.46 us (7%)
  between operations  0.64 us (3%)
    pallas_call x1, Pallas kernels, on_device(): pl.pallas_call(functools.partial(kernel, sizes, cx, cy, cz, lanes), out_s...  19.5 us
    squeeze x1, local copies, waits for them, and re-layouts, on_device(): return (both[0], both[1])  1.46 us

profile of v5, /device:TPU:0, one launch (start us, length us, event | category | flops | bytes accessed | tf_op | source)
XLA Modules:
  0.0 21.6 jit_solution(11957647085566623037)
XLA Ops:
  0.6 19.5 %shard_map.68 = f32[2,3,4,8,128]{4,3,2,1,0:T(8,128)} custom-call(f32[6,12,192]{2,1,0:T(8,128)} %energy_hbm.1, f32[2,4,64]{2,1,0:T(4,128)} %density_hbm.1, s32[2,4,64]{2,1,0:T(4,128)} %region_hbm.1, f32[3]{0:T(128)} %gamma_hbm.1, f32[368,160]{1,0:T(8,128)} %constant.2.clone.plane_hbm), custom_call_target="tpu_custom_call" | custom-call | tf_op jit(solution)/shard_map/pallas_call | solution.py:651
  20.1 1.5 %slice_bitcast_fusion = (f32[3,4,8,128]{3,2,1,0:T(8,128)}, f32[3,4,8,128]{3,2,1,0:T(8,128)}) fusion(f32[2,3,4,8,128]{4,3,2,1,0:T(8,128)} %shard_map.68), kind=kLoop, calls=%fused_computation | loop fusion | bytes 196608 | tf_op jit(solution)/shard_map/squeeze | solution.py:663

commit v6 on v5

--- a/solution.py
+++ b/solution.py
@@ -515,10 +515,10 @@
 
     if sum(group_size(stage, sizes) - 1 for stage in stages):
         pl.semaphore_wait(barrier, sum(group_size(stage, sizes) - 1 for stage in stages))
-    start(0)
     if dirs[2]:
         pack_z()
         each_z(lambda a, b, c: copy_z(a, b, c, False).start())
+    start(0)
     finish(0)
 
     @pl.loop(0, PHASES - 1)

time: 21.8 us -> 21.8 us (level)
  no operation moved by 1% of the time
where the time goes in v6:
time: 21.8 us; the launch traced here: 21.6 us
  Pallas kernels  19.5 us (89%)
  local copies, waits for them, and re-layouts  1.46 us (7%)
  between operations  0.64 us (3%)
    pallas_call x1, Pallas kernels, on_device(): pl.pallas_call(functools.partial(kernel, sizes, cx, cy, cz, lanes), out_s...  19.5 us
    squeeze x1, local copies, waits for them, and re-layouts, on_device(): return (both[0], both[1])  1.46 us

profile of v6, /device:TPU:0, one launch (start us, length us, event | category | flops | bytes accessed | tf_op | source)
XLA Modules:
  0.0 21.6 jit_solution(12213593047932145428)
XLA Ops:
  0.6 19.5 %shard_map.68 = f32[2,3,4,8,128]{4,3,2,1,0:T(8,128)} custom-call(f32[6,12,192]{2,1,0:T(8,128)} %energy_hbm.1, f32[2,4,64]{2,1,0:T(4,128)} %density_hbm.1, s32[2,4,64]{2,1,0:T(4,128)} %region_hbm.1, f32[3]{0:T(128)} %gamma_hbm.1, f32[368,160]{1,0:T(8,128)} %constant.2.clone.plane_hbm), custom_call_target="tpu_custom_call" | custom-call | tf_op jit(solution)/shard_map/pallas_call | solution.py:651
  20.1 1.5 %slice_bitcast_fusion = (f32[3,4,8,128]{3,2,1,0:T(8,128)}, f32[3,4,8,128]{3,2,1,0:T(8,128)}) fusion(f32[2,3,4,8,128]{4,3,2,1,0:T(8,128)} %shard_map.68), kind=kLoop, calls=%fused_computation | loop fusion | bytes 196608 | tf_op jit(solution)/shard_map/squeeze | solution.py:663
